TPU v7x, 32 devices: a whole 2x2x4 slice. The times are simulated.
32 devices in a mesh: dp: 8 (over z, y), group: 4 (over x, core).
Axes of the slice: x: 2, y: 2, z: 4, core: 2. Of those that a mesh axis runs over, the one named last changes fastest.
Arguments:
- gradients: bfloat16 [32, 2, 2048, 512], P(('dp', 'group'))
- errors: float32 [32, 2, 2048, 512], P(('dp', 'group')), may hold values from -4 to 4
- warm_right: float32 [2, 512, 32], replicated, may hold values from -6 to 6
- norm_grads: float32 [32, 2, 2048], P(('dp', 'group'))
- norm_weights: float32 [2, 2048], replicated, may hold values from 0.5 to 1.5
- norm_moment: float32 [2, 2048], replicated, may hold values from -4 to 4
- owners: int32 [32], replicated, may hold values from 0 to 31, as said below
- slot_weights: bfloat16 [32, 2, 128, 512], P(('dp', 'group')), may hold values from -6 to 6
- slot_moment: float32 [32, 2, 128, 512], P(('dp', 'group')), may hold values from -4 to 4
Outputs:
- new_errors: float32 [32, 2, 2048, 512], P(('dp', 'group'))
- new_slot_moment: float32 [32, 2, 128, 512], P(('dp', 'group'))
- new_weights: bfloat16 [2, 2048, 512], replicated
- new_norm_weights: float32 [2, 2048], replicated
- new_norm_moment: float32 [2, 2048], replicated
Inputs may be any that keep to these rules, and one draw needn't show every extreme that they name: `owners`: each replica owns at most 2 pieces and some replica owns exactly 2; a replica's pieces occupy its slots in increasing piece order, the other slots hold nothing that is read.
All inputs are finite; a program needn't handle non-finite values.
Results may differ from a plain program's by a relative error of at most 0.0004.
Values may be sent and summed in bfloat16 or wider, within the bound.
A program may use at most 128 MiB of HBM per device.

v0:
```python
import jax
import jax.numpy as jnp
from jax import lax
from jax.sharding import PartitionSpec as P

momentum_decay = 0.9
step_rate = 0.5


def orthonormal(factor):
    gram = jnp.einsum("...dr,...ds->...rs", factor, factor, precision=lax.Precision.HIGHEST)
    lower_factor = jnp.linalg.cholesky(gram)
    solved = jax.scipy.linalg.solve_triangular(
        lower_factor, jnp.swapaxes(factor, -1, -2), lower=True
    )
    return jnp.swapaxes(solved, -1, -2)


def times_right(merged, right_basis):
    return jnp.einsum("...dk,...kr->...dr", merged, right_basis, precision=lax.Precision.HIGHEST)


def times_left(merged, left_basis):
    return jnp.einsum("...dk,...dr->...kr", merged, left_basis, precision=lax.Precision.HIGHEST)


def stacked_rounds(merged, warm_right, norm_local, replicas):
    left_sum, norm_sum = lax.psum((times_right(merged, warm_right), norm_local), ("dp", "group"))
    left_one = orthonormal(left_sum)
    right_one = lax.psum(times_left(merged, left_one), ("dp", "group")) / replicas
    left_two = orthonormal(lax.psum(times_right(merged, right_one), ("dp", "group")))
    right_two = lax.psum(times_left(merged, left_two), ("dp", "group")) / replicas
    return (left_two, right_two, norm_sum)


def on_device(
    gradients,
    errors,
    warm_right,
    norm_grads,
    norm_weights,
    norm_moment,
    owners,
    slot_weights,
    slot_moment,
):
    replicas = lax.axis_size(("dp", "group"))
    merged = gradients[0].astype(jnp.float32) + errors[0]
    left_two, right_two, norm_sum = stacked_rounds(merged, warm_right, norm_grads[0], replicas)
    update = jnp.einsum("mdr,mkr->mdk", left_two, right_two, precision=lax.Precision.HIGHEST)
    new_errors = (merged - update)[None]
    new_norm_moment = momentum_decay * norm_moment + norm_sum / replicas
    new_norm_weights = norm_weights - step_rate * new_norm_moment
    piece_count = owners.shape[0]
    slot_count = slot_moment.shape[1]
    piece_rows = slot_moment.shape[2]
    features = slot_moment.shape[3]
    positions = jnp.arange(piece_count, dtype=jnp.int32)
    same_owner = owners[:, None] == owners[None, :]
    earlier = positions[:, None] < positions[None, :]
    slot_of = jnp.sum((same_owner & earlier).astype(jnp.int32), axis=0)
    my_index = lax.axis_index(("dp", "group"))
    owned = owners == my_index
    slot_range = jnp.arange(slot_count, dtype=jnp.int32)
    selector = (owned[:, None] & (slot_of[:, None] == slot_range[None, :])).astype(jnp.float32)
    pieces = update.reshape(piece_count, piece_rows, features)
    slot_update = jnp.einsum("js,jrk->srk", selector, pieces, precision=lax.Precision.HIGHEST)
    used = jnp.sum(selector, axis=0)[:, None, None] > 0.5
    old_moment = slot_moment[0]
    moment_slots = jnp.where(used, momentum_decay * old_moment + slot_update, old_moment)
    weight_slots = (slot_weights[0].astype(jnp.float32) - step_rate * moment_slots).astype(
        jnp.bfloat16
    )
    every_slot = lax.all_gather(weight_slots[None], ("dp", "group"), axis=0, tiled=True)
    chosen = every_slot[owners, slot_of]
    new_weights = chosen.reshape(2, piece_count * piece_rows // 2, features)
    return (new_errors, moment_slots[None], new_weights, new_norm_weights, new_norm_moment)


def solution(mesh):
    placed = (
        P(("dp", "group"), None, None, None),
        P(("dp", "group"), None, None, None),
        P(),
        P(("dp", "group"), None, None),
        P(),
        P(),
        P(),
        P(("dp", "group"), None, None, None),
        P(("dp", "group"), None, None, None),
    )
    return jax.shard_map(
        on_device,
        mesh=mesh,
        in_specs=placed,
        out_specs=(
            P(("dp", "group"), None, None, None),
            P(("dp", "group"), None, None, None),
            P(),
            P(),
            P(),
        ),
        check_vma=False,
    )
```

profile of v0, /device:TPU:0, one launch (start us, length us, event | category | flops | bytes accessed | tf_op | source)
XLA Modules:
  0.0 692.3 jit_solution(12176303212669192106)
XLA Ops:
  8.1 11.7 %fusion.6 = f32[2,2048,32]{1,2,0:T(8,128)} fusion(f32[2,512,32]{1,2,0:T(8,128)S(1)} %copy-done, f32[1,2,2048,512]{3,2,1,0:T(8,128)} %param.13, bf16[1,2,2048,512]{3,2,1,0:T(8,128)(2,1)} %param.12), kind=kOutput, calls=%fused_computation.8 | convolution fusion | flops 809500672 | bytes 13238272 | tf_op jit(solution)/shard_map/...dk,...kr->...dr/dot_general | solution.py:20
  19.9 130.6 %all-reduce.5.cloned.1.call-done = f32[2,2048,32]{1,2,0:T(8,128)} async-done(((f32[2,2048,32]{1,2,0:T(8,128)}), f32[2,2048,32]{1,2,0:T(8,128)}) %all-reduce.5.cloned.1.call-update) | async-done | bytes 524304 | tf_op jit(solution)/shard_map/psum | solution.py:28
  150.5 1.8 fusion.44
  152.4 5.9 custom-call.10
  158.5 4.9 custom-call.11
  163.4 1.7 fusion.20
  165.1 9.1 %fusion.4 = f32[2,512,32]{1,2,0:T(8,128)} fusion(f32[2,32,2048]{2,1,0:T(8,128)S(1)} %fusion.20, f32[1,2,2048,512]{3,2,1,0:T(8,128)} %param.13, bf16[1,2,2048,512]{3,2,1,0:T(8,128)(2,1)} %param.12), kind=kOutput, calls=%fused_computation.6 | convolution fusion | flops 809500672 | bytes 13238272 | tf_op jit(solution)/shard_map/...dk,...dr->...kr/dot_general | solution.py:24
  174.5 121.4 %all-reduce.7.cloned.1.call-done = f32[2,512,32]{1,2,0:T(8,128)} async-done(((f32[2,512,32]{1,2,0:T(8,128)}), f32[2,512,32]{1,2,0:T(8,128)}) %all-reduce.7.cloned.1.call-update) | async-done | bytes 131088 | tf_op jit(solution)/shard_map/psum | solution.py:30
  295.9 13.6 %fusion.2 = f32[2,2048,32]{1,2,0:T(8,128)} fusion(f32[2,512,32]{1,2,0:T(8,128)} %all-reduce.7.cloned.1.call-done, f32[1,2,2048,512]{3,2,1,0:T(8,128)} %param.13, bf16[1,2,2048,512]{3,2,1,0:T(8,128)(2,1)} %param.12), kind=kOutput, calls=%fused_computation.4 | convolution fusion | flops 809533440 | bytes 13238272 | tf_op jit(solution)/shard_map/...dk,...kr->...dr/dot_general | solution.py:20
  309.8 126.8 %all-reduce.9.cloned.1.call-done = f32[2,2048,32]{1,2,0:T(8,128)} async-done(((f32[2,2048,32]{1,2,0:T(8,128)}), f32[2,2048,32]{1,2,0:T(8,128)}) %all-reduce.9.cloned.1.call-update) | async-done | bytes 524304 | tf_op jit(solution)/shard_map/psum | solution.py:31
  436.6 1.8 fusion.45
  438.4 5.9 custom-call.12
  444.5 4.9 custom-call.13
  449.5 1.7 fusion.18
  451.2 9.1 %fusion = f32[2,512,32]{1,2,0:T(8,128)} fusion(f32[2,32,2048]{2,1,0:T(8,128)S(1)} %fusion.18, f32[1,2,2048,512]{3,2,1,0:T(8,128)} %param.13, bf16[1,2,2048,512]{3,2,1,0:T(8,128)(2,1)} %param.12), kind=kOutput, calls=%fused_computation.2 | convolution fusion | flops 809500672 | bytes 13238272 | tf_op jit(solution)/shard_map/...dk,...dr->...kr/dot_general | solution.py:24
  460.7 121.2 %all-reduce.11.cloned.1.call-done = f32[2,512,32]{1,2,0:T(8,128)} async-done(((f32[2,512,32]{1,2,0:T(8,128)}), f32[2,512,32]{1,2,0:T(8,128)}) %all-reduce.11.cloned.1.call-update) | async-done | bytes 131088 | tf_op jit(solution)/shard_map/psum | solution.py:32
  581.9 7.7 %fusion.22 = f32[2,2048,512]{2,1,0:T(8,128)S(1)} fusion(f32[2,32,2048]{2,1,0:T(8,128)S(1)} %fusion.18, f32[2,512,32]{1,2,0:T(8,128)} %all-reduce.11.cloned.1.call-done), kind=kOutput, calls=%fused_computation.23 | convolution fusion | flops 805339136 | bytes 9043968 | tf_op jit(solution)/shard_map/mdr,mkr->mdk/dot_general | solution.py:50
  589.6 3.4 copy-done.1
  593.0 8.5 %fusion.17 = (bf16[2,128,512]{2,0,1:T(2,128)(2,1)S(1)}, f32[2,128,512]{2,0,1:T(2,128)S(1)}) fusion(bf16[1,2,128,512]{3,2,1,0:T(8,128)(2,1)S(1)} %copy-done.3, f32[32,128,512]{2,1,0:T(8,128)S(1)} %bitcast.76, pred[32]{0:T(512)(128)(4,1)S(1)} %broadcast_compare_fusion.1, s32[32]{0:T(128)S(1)} %convert_reduce_fusion, f32[1,2,128,512]{3,2,1,0:T(8,128)S(1)} %copy-done.2, ...), kind=kOutput, calls=%fused_computation.17 | convolution fusion | flops 51249280 | bytes 9961634 | tf_op jit(solution)/shard_map/js,jrk->srk/dot_general | solution.py:67
  602.2 40.1 %psum.39 = f32[2,2048]{1,0:T(2,128)S(1)} all-reduce(f32[2,2048]{1,0:T(2,128)S(1)} %bitcast.80), channel_id=1, replica_groups=mesh['dp'=8,'group'=4] {'dp','group'}, use_global_device_ids=true, to_apply=%region_8.11 | all-reduce | flops 4096 | bytes 32768 | tf_op jit(solution)/shard_map/psum | solution.py:28
  643.0 0.9 copy.47
  643.8 13.9 %fusion.8 = f32[1,2,2048,512]{3,2,1,0:T(8,128)} fusion(f32[2,2048,512]{2,1,0:T(8,128)} %copy-done.1, f32[1,2,2048,512]{3,2,1,0:T(8,128)} %param.13, bf16[1,2,2048,512]{3,2,1,0:T(8,128)(2,1)} %param.12), kind=kLoop, calls=%fused_computation.10 | loop fusion | flops 6291456 | bytes 29360128 | tf_op jit(solution)/shard_map/broadcast_in_dim | solution.py:51
  657.8 21.3 %all-gather.3.cloned.1.call-done = bf16[64,128,512]{2,1,0:T(8,128)(2,1)} async-done(((bf16[2,128,512]{2,1,0:T(8,128)(2,1)}), bf16[64,128,512]{2,1,0:T(8,128)(2,1)}) %all-gather.3.cloned.1.call-update) | async-done | bytes 8388624 | tf_op jit(solution)/shard_map/all_gather | solution.py:74
  679.1 6.2 gather_fusion
  (44 shorter events, 3.8 us)
Async XLA Ops:
  7.2 0.9 copy-start
  7.2 143.3 %all-reduce.5.cloned.1.call-start = ((), (), s32[]{:S(2)}) async-start(), calls=%async_computation | async-start | bytes 1048576 | tf_op jit(solution)/shard_map/psum | solution.py:28
  19.8 276.0 %all-reduce.7.cloned.1.call-start = ((), (), s32[]{:S(2)}) async-start(), calls=%async_computation.1 | async-start | bytes 262144 | tf_op jit(solution)/shard_map/psum | solution.py:30
  174.2 135.3 %copy-start.7 = (s32[32]{0:T(128)S(1)}, s32[32]{0:T(128)}, u32[]{:S(2)}) copy-start(s32[32]{0:T(128)} %param.18) | copy-start | bytes 388
  174.3 262.3 %all-reduce.9.cloned.1.call-start = ((), (), s32[]{:S(2)}) async-start(), calls=%async_computation.2 | async-start | bytes 1048576 | tf_op jit(solution)/shard_map/psum | solution.py:31
  309.5 272.4 %all-reduce.11.cloned.1.call-start = ((), (), s32[]{:S(2)}) async-start(), calls=%async_computation.3 | async-start | bytes 262144 | tf_op jit(solution)/shard_map/psum | solution.py:32
  451.2 141.8 %copy-start.2 = (f32[1,2,128,512]{3,2,1,0:T(8,128)S(1)}, f32[1,2,128,512]{3,2,1,0:T(8,128)}, u32[]{:S(2)}) copy-start(f32[1,2,128,512]{3,2,1,0:T(8,128)} %param.20) | copy-start | bytes 1572868
  451.2 141.8 %copy-start.3 = (bf16[1,2,128,512]{3,2,1,0:T(8,128)(2,1)S(1)}, bf16[1,2,128,512]{3,2,1,0:T(8,128)(2,1)}, u32[]{:S(2)}) copy-start(bf16[1,2,128,512]{3,2,1,0:T(8,128)(2,1)} %param.19) | copy-start | bytes 786436
  460.3 218.7 %all-gather.3.cloned.1.call-start = ((), (), s32[]{:S(2)}) async-start(), calls=%async_computation.4 | async-start | bytes 8650752 | tf_op jit(solution)/shard_map/all_gather | solution.py:74
  460.6 141.6 %copy-start.6 = (f32[1,2,2048]{2,1,0:T(2,128)S(1)}, f32[1,2,2048]{2,1,0:T(2,128)}, u32[]{:S(2)}) copy-start(f32[1,2,2048]{2,1,0:T(2,128)} %param.15) | copy-start | bytes 49156
  460.6 181.7 %copy-start.4 = (f32[2,2048]{1,0:T(2,128)S(1)}, f32[2,2048]{1,0:T(2,128)}, u32[]{:S(2)}) copy-start(f32[2,2048]{1,0:T(2,128)} %param.16) | copy-start | bytes 49156
  460.6 181.7 %copy-start.5 = (f32[2,2048]{1,0:T(2,128)S(1)}, f32[2,2048]{1,0:T(2,128)}, u32[]{:S(2)}) copy-start(f32[2,2048]{1,0:T(2,128)} %param.17) | copy-start | bytes 49156
  589.6 3.4 copy-start.1
Sparse Core Ops, SparseCore 0:
  20.0 130.5 all-reduce.4
  174.4 121.4 all-reduce.6
  309.6 126.8 all-reduce.8
  460.5 121.3 all-reduce.10
  602.3 76.7 all-gather.2
where the time goes:
time: 698 us; the launch traced here: 692 us
  waiting for transfers between devices  521 us (75%)
  matrix products  66.7 us (10%)
  blocking collectives  40.1 us (6%)
  other arithmetic  36.8 us (5%)
  between operations  14.4 us (2%)
  local copies, waits for them, and re-layouts  12.3 us (2%)
    psum x1, waiting for transfers between devices, stacked_rounds(): lax.psum((times_right(merged, warm_right), norm_local), ('dp', 'group'))  131 us
    psum x1, waiting for transfers between devices, stacked_rounds(): lax.psum(times_right(merged, right_one), ('dp', 'group'))  127 us
    psum x1, waiting for transfers between devices, stacked_rounds(): lax.psum(times_left(merged, left_one), ('dp', 'group')) / replicas  121 us
    psum x1, waiting for transfers between devices, stacked_rounds(): lax.psum(times_left(merged, left_two), ('dp', 'group')) / replicas  121 us
    psum x1, blocking collectives, stacked_rounds(): lax.psum((times_right(merged, warm_right), norm_local), ('dp', 'group'))  40.1 us
    dot_general x2, matrix products, times_right(): jnp.einsum('...dk,...kr->...dr', merged, right_basis, precision=lax.Preci...  25.4 us
    all_gather x1, waiting for transfers between devices, on_device(): lax.all_gather(weight_slots[None], ('dp', 'group'), axis=0, tiled=True)  21.3 us
    dot_general x2, matrix products, times_left(): jnp.einsum('...dk,...dr->...kr', merged, left_basis, precision=lax.Precis...  18.3 us
  transfers between devices with their start and end apart: 5, of which 5 were waited for; matrix products, arithmetic and copies ran while one was open for 2% of the time, Pallas kernels for 0%

commit v1 on v0

v1 whole, which is shorter than its diff:
```python
import functools

import jax
import jax.numpy as jnp
from jax import lax
from jax.experimental import pallas as pl
from jax.experimental.pallas import tpu as pltpu
from jax.sharding import PartitionSpec as P

momentum_decay = 0.9
step_rate = 0.5
MESH = pl.DeviceIdType.MESH
AXES = ("dp", "group")
F32 = jnp.float32
BF16 = jnp.bfloat16
NT = (((1,), (1,)), ((), ()))
NN = (((1,), (0,)), ((), ()))
TN = (((0,), (0,)), ((), ()))
BLOCK = 256


def split(value):
    high = value.astype(BF16)
    return high, (value - high.astype(F32)).astype(BF16)


def bits_of(sizes):
    return [
        [(axis, 1 << b) for b in range(sizes[axis].bit_length() - 1)] for axis in AXES
    ]


def stages_of(sizes, first):
    dp, group = bits_of(sizes)
    near = group + dp[:1]
    rest = dp[1:]
    stages = [near[:1], near[1:]] if first else [near]
    stages += [rest[i : i + 2] for i in range(0, len(rest), 2)]
    return [s for s in stages if s]


def plan_of(stages, tiles):
    plan = []
    held = tiles
    for stage in stages:
        members = 1 << len(stage)
        scatter = held % members == 0
        after = held // members if scatter else held
        plan.append((members, scatter, held, after))
        held = after
    return plan


def peer_of(coords, stage, d):
    out = dict(coords)
    for i, (axis, weight) in enumerate(stage):
        if (d >> i) & 1:
            bit = (coords[axis] // weight) % 2
            out[axis] = out[axis] + weight * (1 - 2 * bit)
    return tuple(out[axis] for axis in AXES)


def place_of(coords, stage, d):
    place = 0
    for i, (axis, weight) in enumerate(stage):
        bit = (coords[axis] // weight) % 2
        if (d >> i) & 1:
            bit = 1 - bit
        place = place + bit * (1 << i)
    return place


def sum_over(coords, stages, plan, part, full, recv, send_sems, recv_sems, works=()):
    works = list(works)
    base = 0
    slot = 0
    sem = 0
    bases = []

    def work():
        if works:
            works.pop(0)()

    for stage, (members, scatter, held, after) in zip(stages, plan):
        copies = []
        bases.append(base)
        for d in range(1, members):
            start = base + place_of(coords, stage, d) * after if scatter else base
            copy = pltpu.make_async_remote_copy(
                src_ref=part.at[pl.ds(start, after)],
                dst_ref=recv.at[pl.ds(slot + (d - 1) * after, after)],
                send_sem=send_sems.at[sem],
                recv_sem=recv_sems.at[sem],
                device_id=peer_of(coords, stage, d),
                device_id_type=MESH,
            )
            copy.start()
            copies.append(copy)
            sem += 1
        work()
        if scatter:
            base = base + place_of(coords, stage, 0) * after
        for copy in copies:
            copy.wait()
        total = part[pl.ds(base, after)]
        for d in range(1, members):
            total = total + recv[pl.ds(slot + (d - 1) * after, after)]
        part[pl.ds(base, after)] = total
        slot += (members - 1) * after
    full[pl.ds(base, after)] = part[pl.ds(base, after)]
    for stage, (members, scatter, held, after), before in reversed(
        list(zip(stages, plan, bases))
    ):
        if not scatter:
            continue
        copies = []
        for d in range(1, members):
            copy = pltpu.make_async_remote_copy(
                src_ref=full.at[pl.ds(base, after)],
                dst_ref=full.at[pl.ds(base, after)],
                send_sem=send_sems.at[sem],
                recv_sem=recv_sems.at[sem],
                device_id=peer_of(coords, stage, d),
                device_id_type=MESH,
            )
            copy.start()
            copies.append(copy)
            sem += 1
        work()
        for copy in copies:
            copy.wait()
        base = before
    while works:
        work()


def tiles_to_wide(tiles, rank):
    per = rank // 8
    count = tiles.shape[0] // per
    blocks = tiles.reshape(count, rank, 128)
    return jnp.concatenate([blocks[i] for i in range(count)], axis=1)


def wide_to_tiles(wide, rank):
    per = rank // 8
    count = wide.shape[1] // 128
    return jnp.concatenate(
        [wide[:, i * 128 : (i + 1) * 128].reshape(per, 8, 128) for i in range(count)],
        axis=0,
    )


def rounds_kernel(
    sizes,
    grads,
    errs,
    warm,
    left_out,
    right_out,
    e_buf,
    g_buf,
    high,
    low,
    l_part_a,
    l_full_a,
    l_recv_a,
    l_part_b,
    l_full_b,
    l_recv_b,
    r_part_a,
    r_full_a,
    r_recv_a,
    r_part_b,
    r_full_b,
    r_recv_b,
    chol,
    load_sems,
    l_send,
    l_got,
    r_send,
    r_got,
):
    replicas = sizes["dp"] * sizes["group"]
    mats, rank, features = warm.shape
    rows = e_buf.shape[0]
    per_mat = rows // mats
    steps = rows // BLOCK
    mat_steps = per_mat // BLOCK
    l_tiles = l_part_a.shape[0]
    r_tiles = r_part_a.shape[0]
    coords = {axis: lax.axis_index(axis) for axis in AXES}
    l_stages, r_stages = stages_of(sizes, True), stages_of(sizes, False)
    l_plan, r_plan = plan_of(l_stages, l_tiles), plan_of(r_stages, r_tiles)

    def load(step):
        span = pl.ds(step * BLOCK, BLOCK)
        return (
            pltpu.make_async_copy(errs.at[span], e_buf.at[span], load_sems.at[0, step]),
            pltpu.make_async_copy(grads.at[span], g_buf.at[span], load_sems.at[1, step]),
        )

    def begin(step, carry):
        for copy in load(step):
            copy.start()
        return carry

    lax.fori_loop(0, steps, begin, 0)

    barrier = pltpu.get_barrier_semaphore()
    seen = []
    for stage in l_stages + r_stages:
        for d in range(1, 1 << len(stage)):
            key = tuple(stage[i] for i in range(len(stage)) if (d >> i) & 1)
            if key not in seen:
                seen.append(key)
                pl.semaphore_signal(
                    barrier,
                    inc=1,
                    device_id=peer_of(coords, stage, d),
                    device_id_type=MESH,
                )
    pl.semaphore_wait(barrier, len(seen))

    tiles_per_block = l_tiles // steps

    def left_block(step, m_high, m_low, right, part):
        stacked, right_high = right
        wide = lax.dot_general(stacked, m_high, NT, preferred_element_type=F32)
        value = wide[:rank] + wide[rank:]
        value = value + lax.dot_general(right_high, m_low, NT, preferred_element_type=F32)
        part[pl.ds(step * tiles_per_block, tiles_per_block)] = wide_to_tiles(value, rank)

    def stack(right):
        right_high, right_low = split(right)
        return jnp.concatenate([right_high, right_low], axis=0), right_high

    for m in range(mats):
        right = stack(warm[m])

        def first(i, carry):
            step = m * mat_steps + i
            span = pl.ds(step * BLOCK, BLOCK)
            for copy in load(step):
                copy.wait()
            merged = g_buf[span].astype(F32) + e_buf[span]
            m_high, m_low = split(merged)
            high[span] = m_high
            low[span] = m_low
            left_block(step, m_high, m_low, right, l_part_a)
            return carry

        lax.fori_loop(0, mat_steps, first, 0)

    def left_product(rights, part):
        for m in range(mats):
            right = stack(rights[m])

            def one(i, carry):
                step = m * mat_steps + i
                span = pl.ds(step * BLOCK, BLOCK)
                left_block(step, high[span], low[span], right, part)
                return carry

            lax.fori_loop(0, mat_steps, one, 0)

    mat_r_tiles = r_tiles // mats

    def right_product(full, part):
        for m in range(mats):

            def one(i, total):
                step = m * mat_steps + i
                span = pl.ds(step * BLOCK, BLOCK)
                left = tiles_to_wide(full[pl.ds(step * tiles_per_block, tiles_per_block)], rank)
                stacked, left_high = stack(left)
                wide = lax.dot_general(stacked, high[span], NN, preferred_element_type=F32)
                more = lax.dot_general(left_high, low[span], NN, preferred_element_type=F32)
                return total + (wide[:rank] + wide[rank:] + more)

            total = lax.fori_loop(0, mat_steps, one, jnp.zeros((rank, features), F32))
            part[m * mat_r_tiles : (m + 1) * mat_r_tiles] = wide_to_tiles(total, rank)

    row_index = lax.broadcasted_iota(jnp.int32, (rank, 128), 0)
    lane_index = lax.broadcasted_iota(jnp.int32, (rank, 128), 1)

    def gram(full):
        for m in range(mats):

            def one(i, total):
                step = m * mat_steps + i
                left = tiles_to_wide(full[pl.ds(step * tiles_per_block, tiles_per_block)], rank)
                return total + lax.dot_general(
                    left, left, NT, precision=lax.Precision.HIGHEST, preferred_element_type=F32
                )

            total = lax.fori_loop(0, mat_steps, one, jnp.zeros((rank, rank), F32))
            unit = (lane_index == row_index + rank).astype(F32)
            chol[m] = unit + jnp.concatenate(
                [total, jnp.zeros((rank, 128 - rank), F32)], axis=1
            )

    def eliminate(k, carry):
        out = []
        for value in carry:
            row = jnp.sum(jnp.where(row_index == k, value, 0.0), axis=0, keepdims=True)
            column = jnp.sum(jnp.where(lane_index == k, value, 0.0), axis=1, keepdims=True)
            pivot = jnp.sum(jnp.where(lane_index[:1] == k, row, 0.0), axis=1, keepdims=True)
            factor = jnp.where(row_index > k, column / pivot, 0.0)
            out.append(value - factor * row)
        return tuple(out)

    def eliminate_some(lower, upper):
        values = lax.fori_loop(
            lower, upper, eliminate, tuple(chol[m] for m in range(mats))
        )
        for m in range(mats):
            chol[m] = values[m]

    def inverse_factor(m):
        value = chol[m]
        pivots = jnp.sum(jnp.where(lane_index == row_index, value, 0.0), axis=1, keepdims=True)
        return value[:, rank : 2 * rank] * lax.rsqrt(pivots)

    def works_of(full):
        quarter = rank // 4

        def opening():
            gram(full)
            eliminate_some(0, quarter)

        return [opening] + [
            functools.partial(eliminate_some, i * quarter, (i + 1) * quarter)
            for i in range(1, 4)
        ]

    def exact(a, b, dims):
        return lax.dot_general(
            a, b, dims, precision=lax.Precision.HIGHEST, preferred_element_type=F32
        )

    def right_sum(full, m):
        return tiles_to_wide(full[m * mat_r_tiles : (m + 1) * mat_r_tiles], rank)

    sum_over(coords, l_stages, l_plan, l_part_a, l_full_a, l_recv_a, l_send.at[0], l_got.at[0])
    right_product(l_full_a, r_part_a)
    sum_over(
        coords, r_stages, r_plan, r_part_a, r_full_a, r_recv_a, r_send.at[0], r_got.at[0],
        works_of(l_full_a),
    )
    rights = [
        exact(inverse_factor(m), right_sum(r_full_a, m), NN) / replicas for m in range(mats)
    ]
    left_product(rights, l_part_b)
    sum_over(coords, l_stages, l_plan, l_part_b, l_full_b, l_recv_b, l_send.at[1], l_got.at[1])
    right_product(l_full_b, r_part_b)
    sum_over(
        coords, r_stages, r_plan, r_part_b, r_full_b, r_recv_b, r_send.at[1], r_got.at[1],
        works_of(l_full_b),
    )
    for m in range(mats):
        inverse = inverse_factor(m)
        right_two = exact(inverse, right_sum(r_full_b, m), NN) / replicas
        right_out[m] = right_two
        for i in range(mat_steps):
            step = m * mat_steps + i
            left = tiles_to_wide(
                l_full_b[step * tiles_per_block : (step + 1) * tiles_per_block], rank
            )
            left_out[m, :, i * BLOCK : (i + 1) * BLOCK] = exact(inverse, left, NN)


def rounds(sizes, grads, errs, warm):
    rows, features = errs.shape
    mats, rank, _ = warm.shape
    l_tiles = rows * rank // 1024
    r_tiles = mats * features * rank // 1024
    l_plan = plan_of(stages_of(sizes, True), l_tiles)
    r_plan = plan_of(stages_of(sizes, False), r_tiles)

    def slots(plan):
        return sum((members - 1) * after for members, _, _, after in plan)

    def sems(plan):
        return sum((members - 1) * (2 if scatter else 1) for members, scatter, _, _ in plan)

    def tiles(count):
        return pltpu.VMEM((count, 8, 128), F32)

    l_bufs = [tiles(l_tiles), tiles(l_tiles), tiles(slots(l_plan))]
    r_bufs = [tiles(r_tiles), tiles(r_tiles), tiles(slots(r_plan))]
    return pl.pallas_call(
        functools.partial(rounds_kernel, sizes),
        out_shape=(
            jax.ShapeDtypeStruct((mats, rank, rows // mats), F32),
            jax.ShapeDtypeStruct((mats, rank, features), F32),
        ),
        in_specs=[
            pl.BlockSpec(memory_space=pl.ANY),
            pl.BlockSpec(memory_space=pl.ANY),
            pl.BlockSpec(memory_space=pltpu.VMEM),
        ],
        out_specs=(
            pl.BlockSpec(memory_space=pltpu.VMEM),
            pl.BlockSpec(memory_space=pltpu.VMEM),
        ),
        scratch_shapes=[
            pltpu.VMEM((rows, features), F32),
            pltpu.VMEM((rows, features), BF16),
            pltpu.VMEM((rows, features), BF16),
            pltpu.VMEM((rows, features), BF16),
            *l_bufs,
            *l_bufs,
            *r_bufs,
            *r_bufs,
            pltpu.VMEM((mats, rank, 128), F32),
            pltpu.SemaphoreType.DMA((2, rows // BLOCK)),
            pltpu.SemaphoreType.DMA((2, sems(l_plan))),
            pltpu.SemaphoreType.DMA((2, sems(l_plan))),
            pltpu.SemaphoreType.DMA((2, sems(r_plan))),
            pltpu.SemaphoreType.DMA((2, sems(r_plan))),
        ],
        compiler_params=pltpu.CompilerParams(
            collective_id=0, has_side_effects=True, vmem_limit_bytes=44 * 1024 * 1024
        ),
        name="rounds",
    )(grads, errs, warm)


def finish_kernel(per, slots, places, mine, *refs):
    left, right, grads, errs, moment = refs[:5]
    bases = refs[5 : 5 + per]
    new_errs, weights, new_moment = refs[5 + per :]
    step = pl.program_id(0)
    piece_rows = moment.shape[1]

    @pl.when(step == 0)
    def _():
        new_moment[...] = moment[...]

    l_high, l_low = split(left[0])
    r_high, r_low = split(right[0])
    update = lax.dot_general(
        jnp.concatenate([l_high, l_low, l_high], axis=0),
        jnp.concatenate([r_high, r_high, r_low], axis=0),
        TN,
        preferred_element_type=F32,
    )
    new_errs[...] = (grads[...].astype(F32) + errs[...]) - update
    for i in range(per):
        rows = slice(i * piece_rows, (i + 1) * piece_rows)
        weights[rows] = (bases[i][0] - step_rate * update[rows]).astype(BF16)
        for s in range(slots):

            @pl.when(mine[s] == step * per + i)
            def _():
                new_moment[s] = momentum_decay * moment[s] + update[rows]


def finish(left, right, grads, errs, moment, gathered, places, mine):
    rows, features = errs.shape
    mats, rank, mat_rows = left.shape
    slots, piece_rows, _ = moment.shape
    block = max(BLOCK, piece_rows)
    per = block // piece_rows
    mat_steps = mat_rows // block

    def by_piece(i):
        return pl.BlockSpec(
            (1, piece_rows, features), lambda g, places, mine: (places[g * per + i], 0, 0)
        )

    rows_spec = pl.BlockSpec((block, features), lambda g, places, mine: (g, 0))
    slot_spec = pl.BlockSpec((slots, piece_rows, features), lambda g, places, mine: (0, 0, 0))
    return pl.pallas_call(
        functools.partial(finish_kernel, per, slots),
        out_shape=(
            jax.ShapeDtypeStruct((rows, features), F32),
            jax.ShapeDtypeStruct((rows, features), BF16),
            jax.ShapeDtypeStruct(moment.shape, F32),
        ),
        grid_spec=pltpu.PrefetchScalarGridSpec(
            num_scalar_prefetch=2,
            grid=(rows // block,),
            in_specs=[
                pl.BlockSpec(
                    (1, rank, block),
                    lambda g, places, mine: (g // mat_steps, 0, g % mat_steps),
                ),
                pl.BlockSpec(
                    (1, rank, features), lambda g, places, mine: (g // mat_steps, 0, 0)
                ),
                rows_spec,
                rows_spec,
                slot_spec,
                *[by_piece(i) for i in range(per)],
            ],
            out_specs=(rows_spec, rows_spec, slot_spec),
        ),
        compiler_params=pltpu.CompilerParams(vmem_limit_bytes=40 * 1024 * 1024),
        name="finish",
    )(places, mine, left, right, grads, errs, moment, *([gathered] * per))


def on_device(
    sizes,
    gradients,
    errors,
    warm_right,
    norm_grads,
    norm_weights,
    norm_moment,
    owners,
    slot_weights,
    slot_moment,
):
    replicas = sizes["dp"] * sizes["group"]
    mats, mat_rows, features = gradients.shape[1:]
    slots, piece_rows = slot_moment.shape[1:3]
    piece_count = owners.shape[0]
    base = slot_weights[0].astype(F32) - (step_rate * momentum_decay) * slot_moment[0]
    gathered = lax.all_gather(base, AXES, axis=0, tiled=True)
    norms = lax.all_gather(norm_grads[0].reshape(-1, 128), AXES, axis=0)
    norm_sum = jnp.sum(norms, axis=0).reshape(norm_moment.shape)
    new_norm_moment = momentum_decay * norm_moment + norm_sum / replicas
    new_norm_weights = norm_weights - step_rate * new_norm_moment

    positions = jnp.arange(piece_count, dtype=jnp.int32)
    same_owner = owners[:, None] == owners[None, :]
    earlier = positions[:, None] < positions[None, :]
    slot_of = jnp.sum((same_owner & earlier).astype(jnp.int32), axis=0)
    places = owners * slots + slot_of
    own_places = lax.axis_index(AXES) * slots + jnp.arange(slots, dtype=jnp.int32)
    here = own_places[:, None] == places[None, :]
    mine = jnp.max(jnp.where(here, positions[None, :], -1), axis=1)

    grads = gradients.reshape(mats * mat_rows, features)
    errs = errors.reshape(mats * mat_rows, features)
    left_two, right_two = rounds(sizes, grads, errs, jnp.swapaxes(warm_right, 1, 2))
    new_errors, new_weights, new_moment = finish(
        left_two, right_two, grads, errs, slot_moment[0], gathered, places, mine
    )
    return (
        new_errors.reshape(errors.shape),
        new_moment[None],
        new_weights.reshape(mats, mat_rows, features),
        new_norm_weights,
        new_norm_moment,
    )


def solution(mesh):
    placed = (
        P(AXES, None, None, None),
        P(AXES, None, None, None),
        P(),
        P(AXES, None, None),
        P(),
        P(),
        P(),
        P(AXES, None, None, None),
        P(AXES, None, None, None),
    )
    return jax.shard_map(
        functools.partial(on_device, dict(mesh.shape)),
        mesh=mesh,
        in_specs=placed,
        out_specs=(
            P(AXES, None, None, None),
            P(AXES, None, None, None),
            P(),
            P(),
            P(),
        ),
        check_vma=False,
    )
```

time: 698 us -> 189 us (0.27)
  waiting for transfers between devices: 521 us -> 0.02 us
  Pallas kernels: 0 us -> 115 us
  matrix products: 66.7 us -> 0 us
  other arithmetic: 36.8 us -> 3.01 us
    psum x4 -> x0, waiting for transfers between devices: 500 us -> none  [the longest x1 131 us: stacked_rounds(): lax.psum((times_right(merged, warm_right), norm_local), ('dp', 'group'))]
    pallas_call x0 -> x2, Pallas kernels: none -> 115 us  [the longest x1 100 us: rounds(): pl.pallas_call(functools.partial(rounds_kernel, sizes), out_shape=(jax.Sh...]
    dot_general x8 -> x0, matrix products: 63.4 us -> none  [the longest x2 25.4 us: times_right(): jnp.einsum('...dk,...kr->...dr', merged, right_basis, precision=lax.Preci...]
    all_gather x0 -> x1, blocking collectives: none -> 46.1 us  [on_device(): norms = lax.all_gather(norm_grads[0].reshape(-1, 128), AXES, axis=0)]
    psum x1 -> x0, blocking collectives: 40.1 us -> none  [stacked_rounds(): lax.psum((times_right(merged, warm_right), norm_local), ('dp', 'group'))]
    another operation x12 -> x0, other arithmetic: 22 us -> none  [the longest x7 12 us: orthonormal(): lower_factor = jnp.linalg.cholesky(gram)]
    all_gather x1, waiting for transfers between devices: 21.3 us -> 0.01 us  [on_device(): gathered = lax.all_gather(base, AXES, axis=0, tiled=True)]
    broadcast_in_dim x1 -> x0, other arithmetic: 13.9 us -> none  [on_device(): new_errors = (merged - update)[None]]
  transfers between devices with their start and end apart: 5 -> 1, of which waited for: 5 -> 0; matrix products, arithmetic and copies ran while one was open for 2% -> 1% of each run, Pallas kernels for 0% -> 53%
where the time goes in v1:
time: 189 us; the launch traced here: 188 us
  Pallas kernels  115 us (61%)
  blocking collectives  46.1 us (24%)
  between operations  14.2 us (8%)
  local copies, waits for them, and re-layouts  9.42 us (5%)
  other arithmetic  3.01 us (2%)
    pallas_call x1, Pallas kernels, rounds(): pl.pallas_call(functools.partial(rounds_kernel, sizes), out_shape=(jax.Sh...  100 us
    all_gather x1, blocking collectives, on_device(): norms = lax.all_gather(norm_grads[0].reshape(-1, 128), AXES, axis=0)  46.1 us
    pallas_call x1, Pallas kernels, finish(): pl.pallas_call(functools.partial(finish_kernel, per, slots), out_shape=(j...  15.3 us
    unnamed x16, local copies, waits for them, and re-layouts  8.68 us
  transfers between devices with their start and end apart: 1, of which 0 were waited for; matrix products, arithmetic and copies ran while one was open for 1% of the time, Pallas kernels for 53%

profile of v1, /device:TPU:0, one launch (start us, length us, event | category | flops | bytes accessed | tf_op | source)
XLA Modules:
  0.0 188.2 jit_solution(3329531807723923275)
XLA Ops:
  7.2 0.0 copy-start.3
  7.2 0.0 copy-start.7
  7.2 0.0 copy-start.5
  7.2 0.0 copy-start.6
  7.2 0.0 all-gather.2.cloned.1.call-start
  7.3 2.0 %convert_subtract_fusion = f32[2,128,512]{2,1,0:T(8,128)} fusion(bf16[1,2,128,512]{3,2,1,0:T(8,128)(2,1)} %param.16, f32[1,2,128,512]{3,2,1,0:T(8,128)} %param.17), kind=kLoop, calls=%fused_computation | loop fusion | flops 393216 | bytes 1310720 | tf_op jit(solution)/shard_map/sub | solution.py:520
  9.3 0.0 all-gather.2.cloned.1.call-update
  9.3 0.7 all_gather_reshape_squeeze.3
  10.1 46.1 %all_gather.7 = f32[32,32,128]{2,1,0:T(8,128)S(1)} all-gather(f32[1,32,128]{2,1,0:T(8,128)S(1)} %all_gather_reshape_squeeze.3), channel_id=1, replica_groups=mesh['dp'=8,'group'=4] {'dp','group'}, dimensions={0}, use_global_device_ids=true | all-gather | bytes 540672 | tf_op jit(solution)/shard_map/all_gather | solution.py:522
  56.2 0.0 copy-start.1
  56.2 2.2 %copy-done.1 = bf16[1,2,2048,512]{3,2,1,0:T(8,128)(2,1)S(1)} copy-done((bf16[1,2,2048,512]{3,2,1,0:T(8,128)(2,1)S(1)}, bf16[1,2,2048,512]{3,2,1,0:T(8,128)(2,1)}, u32[]{:S(2)}) %copy-start.1) | copy-done | bytes 4194328
  58.4 0.0 copy-start.4
  58.4 0.9 copy-done.4
  59.3 100.1 %rounds.1 = (f32[2,32,2048]{2,1,0:T(8,128)S(1)}, f32[2,32,512]{2,1,0:T(8,128)S(1)}) custom-call(bf16[4096,512]{1,0:T(8,128)(2,1)S(1)} %bitcast.13, f32[4096,512]{1,0:T(8,128)} %bitcast.11, f32[2,32,512]{2,1,0:T(8,128)S(1)} %bitcast.16), custom_call_target="tpu_custom_call" | custom-call | tf_op jit(solution)/shard_map/rounds/pallas_call | solution.py:391
  159.5 0.0 copy-done.7
  159.5 0.1 convert_reduce_fusion
  159.6 0.2 fusion.1.mine
  159.8 0.0 copy-done.5
  159.8 0.0 copy-done.6
  159.8 0.6 multiply_subtract_fusion
  160.4 0.0 copy-done.3
  160.4 3.4 %copy-done = f32[1,2,2048,512]{3,2,1,0:T(8,128)S(1)} copy-done((f32[1,2,2048,512]{3,2,1,0:T(8,128)S(1)}, f32[1,2,2048,512]{3,2,1,0:T(8,128)}, u32[]{:S(2)}) %copy-start) | copy-done | bytes 8388632
  163.8 2.2 %copy-done.2 = bf16[1,2,2048,512]{3,2,1,0:T(8,128)(2,1)S(1)} copy-done((bf16[1,2,2048,512]{3,2,1,0:T(8,128)(2,1)S(1)}, bf16[1,2,2048,512]{3,2,1,0:T(8,128)(2,1)}, u32[]{:S(2)}) %copy-start.2) | copy-done | bytes 4194328
  166.0 15.3 %finish.1 = (f32[4096,512]{1,0:T(8,128)}, bf16[4096,512]{1,0:T(8,128)(2,1)}, f32[2,128,512]{2,1,0:T(8,128)}) custom-call(s32[32]{0:T(128)S(1)} %multiply_add_fusion.1.places, s32[2]{0:T(128)S(1)} %fusion.1.mine, f32[2,32,2048]{2,1,0:T(8,128)S(1)} %get-tuple-element.10.refs_0_, f32[2,32,512]{2,1,0:T(8,128)S(1)} %get-tuple-element.11.refs_1_, ...), custom_call_target="tpu_custom_call" | custom-call | tf_op jit(solution)/shard_map/finish/pallas_call | solution.py:474
  (8 shorter events, 0.1 us)
Async XLA Ops:
  7.2 153.3 %copy-start.3 = (f32[1,2,128,512]{3,2,1,0:T(8,128)S(1)}, f32[1,2,128,512]{3,2,1,0:T(8,128)}, u32[]{:S(2)}) copy-start(f32[1,2,128,512]{3,2,1,0:T(8,128)} %param.17) | copy-start | bytes 1572868
  7.2 152.3 %copy-start.7 = (s32[32]{0:T(128)S(1)}, s32[32]{0:T(128)}, u32[]{:S(2)}) copy-start(s32[32]{0:T(128)} %param.15) | copy-start | bytes 388
  7.2 152.6 %copy-start.5 = (f32[2,2048]{1,0:T(2,128)S(1)}, f32[2,2048]{1,0:T(2,128)}, u32[]{:S(2)}) copy-start(f32[2,2048]{1,0:T(2,128)} %param.13) | copy-start | bytes 49156
  7.2 152.6 %copy-start.6 = (f32[2,2048]{1,0:T(2,128)S(1)}, f32[2,2048]{1,0:T(2,128)}, u32[]{:S(2)}) copy-start(f32[2,2048]{1,0:T(2,128)} %param.14) | copy-start | bytes 49156
  7.2 153.2 %all-gather.2.cloned.1.call-start = ((), (), s32[]{:S(2)}) async-start(), calls=%async_computation | async-start | bytes 17301504 | tf_op jit(solution)/shard_map/all_gather | solution.py:521
  56.2 2.2 %copy-start.1 = (bf16[1,2,2048,512]{3,2,1,0:T(8,128)(2,1)S(1)}, bf16[1,2,2048,512]{3,2,1,0:T(8,128)(2,1)}, u32[]{:S(2)}) copy-start(bf16[1,2,2048,512]{3,2,1,0:T(8,128)(2,1)} %param.9) | copy-start | bytes 12582916
  58.4 0.9 copy-start.4
  160.4 3.4 %copy-start = (f32[1,2,2048,512]{3,2,1,0:T(8,128)S(1)}, f32[1,2,2048,512]{3,2,1,0:T(8,128)}, u32[]{:S(2)}) copy-start(f32[1,2,2048,512]{3,2,1,0:T(8,128)} %param.10) | copy-start | bytes 25165828
  163.8 2.2 %copy-start.2 = (bf16[1,2,2048,512]{3,2,1,0:T(8,128)(2,1)S(1)}, bf16[1,2,2048,512]{3,2,1,0:T(8,128)(2,1)}, u32[]{:S(2)}) copy-start(bf16[1,2,2048,512]{3,2,1,0:T(8,128)(2,1)} %param.9) | copy-start | bytes 12582916
Sparse Core Ops, SparseCore 0:
  11.5 126.2 all-gather.1

commit v2 on v1

--- a/solution.py
+++ b/solution.py
@@ -155,8 +155,10 @@
     grads,
     errs,
     warm,
+    norms,
     left_out,
     right_out,
+    norm_out,
     e_buf,
     g_buf,
     high,
@@ -187,10 +189,12 @@
     steps = rows // BLOCK
     mat_steps = per_mat // BLOCK
     l_tiles = l_part_a.shape[0]
-    r_tiles = r_part_a.shape[0]
+    sum_tiles = r_part_a.shape[0]
+    r_tiles = mats * features * rank // 1024
+    norm_tiles = norms.shape[0]
     coords = {axis: lax.axis_index(axis) for axis in AXES}
     l_stages, r_stages = stages_of(sizes, True), stages_of(sizes, False)
-    l_plan, r_plan = plan_of(l_stages, l_tiles), plan_of(r_stages, r_tiles)
+    l_plan, r_plan = plan_of(l_stages, l_tiles), plan_of(r_stages, sum_tiles)
 
     def load(step):
         span = pl.ds(step * BLOCK, BLOCK)
@@ -221,6 +225,12 @@
                 )
     pl.semaphore_wait(barrier, len(seen))
 
+    for part in (r_part_a, r_part_b):
+        part[r_tiles : r_tiles + norm_tiles] = norms[...]
+        if sum_tiles > r_tiles + norm_tiles:
+            left_over = sum_tiles - r_tiles - norm_tiles
+            part[r_tiles + norm_tiles :] = jnp.zeros((left_over, 8, 128), F32)
+
     tiles_per_block = l_tiles // steps
 
     def left_block(step, m_high, m_low, right, part):
@@ -357,6 +367,7 @@
         coords, r_stages, r_plan, r_part_b, r_full_b, r_recv_b, r_send.at[1], r_got.at[1],
         works_of(l_full_b),
     )
+    norm_out[...] = r_full_a[r_tiles : r_tiles + norm_tiles]
     for m in range(mats):
         inverse = inverse_factor(m)
         right_two = exact(inverse, right_sum(r_full_b, m), NN) / replicas
@@ -369,11 +380,12 @@
             left_out[m, :, i * BLOCK : (i + 1) * BLOCK] = exact(inverse, left, NN)
 
 
-def rounds(sizes, grads, errs, warm):
+def rounds(sizes, grads, errs, warm, norms):
     rows, features = errs.shape
     mats, rank, _ = warm.shape
     l_tiles = rows * rank // 1024
-    r_tiles = mats * features * rank // 1024
+    r_tiles = mats * features * rank // 1024 + norms.shape[0]
+    r_tiles = (r_tiles + 7) // 8 * 8
     l_plan = plan_of(stages_of(sizes, True), l_tiles)
     r_plan = plan_of(stages_of(sizes, False), r_tiles)
 
@@ -393,13 +405,16 @@
         out_shape=(
             jax.ShapeDtypeStruct((mats, rank, rows // mats), F32),
             jax.ShapeDtypeStruct((mats, rank, features), F32),
+            jax.ShapeDtypeStruct(norms.shape, F32),
         ),
         in_specs=[
             pl.BlockSpec(memory_space=pl.ANY),
             pl.BlockSpec(memory_space=pl.ANY),
             pl.BlockSpec(memory_space=pltpu.VMEM),
+            pl.BlockSpec(memory_space=pltpu.VMEM),
         ],
         out_specs=(
+            pl.BlockSpec(memory_space=pltpu.VMEM),
             pl.BlockSpec(memory_space=pltpu.VMEM),
             pl.BlockSpec(memory_space=pltpu.VMEM),
         ),
@@ -420,10 +435,10 @@
             pltpu.SemaphoreType.DMA((2, sems(r_plan))),
         ],
         compiler_params=pltpu.CompilerParams(
-            collective_id=0, has_side_effects=True, vmem_limit_bytes=44 * 1024 * 1024
+            collective_id=0, has_side_effects=True, vmem_limit_bytes=56 * 1024 * 1024
         ),
         name="rounds",
-    )(grads, errs, warm)
+    )(grads, errs, warm, norms)
 
 
 def finish_kernel(per, slots, places, mine, *refs):
@@ -460,7 +475,7 @@
     rows, features = errs.shape
     mats, rank, mat_rows = left.shape
     slots, piece_rows, _ = moment.shape
-    block = max(BLOCK, piece_rows)
+    block = max(2 * BLOCK, piece_rows)
     per = block // piece_rows
     mat_steps = mat_rows // block
 
@@ -496,7 +511,7 @@
             ],
             out_specs=(rows_spec, rows_spec, slot_spec),
         ),
-        compiler_params=pltpu.CompilerParams(vmem_limit_bytes=40 * 1024 * 1024),
+        compiler_params=pltpu.CompilerParams(vmem_limit_bytes=58 * 1024 * 1024),
         name="finish",
     )(places, mine, left, right, grads, errs, moment, *([gathered] * per))
 
@@ -518,11 +533,8 @@
     slots, piece_rows = slot_moment.shape[1:3]
     piece_count = owners.shape[0]
     base = slot_weights[0].astype(F32) - (step_rate * momentum_decay) * slot_moment[0]
-    gathered = lax.all_gather(base, AXES, axis=0, tiled=True)
-    norms = lax.all_gather(norm_grads[0].reshape(-1, 128), AXES, axis=0)
-    norm_sum = jnp.sum(norms, axis=0).reshape(norm_moment.shape)
-    new_norm_moment = momentum_decay * norm_moment + norm_sum / replicas
-    new_norm_weights = norm_weights - step_rate * new_norm_moment
+    gathered = lax.all_gather(base[None], AXES, axis=0, tiled=True)
+    gathered = gathered.reshape(replicas * slots, piece_rows, features)
 
     positions = jnp.arange(piece_count, dtype=jnp.int32)
     same_owner = owners[:, None] == owners[None, :]
@@ -535,7 +547,12 @@
 
     grads = gradients.reshape(mats * mat_rows, features)
     errs = errors.reshape(mats * mat_rows, features)
-    left_two, right_two = rounds(sizes, grads, errs, jnp.swapaxes(warm_right, 1, 2))
+    left_two, right_two, norm_sum = rounds(
+        sizes, grads, errs, jnp.swapaxes(warm_right, 1, 2), norm_grads.reshape(-1, 8, 128)
+    )
+    norm_sum = norm_sum.reshape(norm_moment.shape)
+    new_norm_moment = momentum_decay * norm_moment + norm_sum / replicas
+    new_norm_weights = norm_weights - step_rate * new_norm_moment
     new_errors, new_weights, new_moment = finish(
         left_two, right_two, grads, errs, slot_moment[0], gathered, places, mine
     )

time: 189 us -> 164 us (0.87)
  blocking collectives: 46.1 us -> 0 us
  waiting for transfers between devices: 0.02 us -> 16.9 us
  Pallas kernels: 115 us -> 127 us
  local copies, waits for them, and re-layouts: 9.42 us -> 1.37 us
    all_gather x1 -> x0, blocking collectives: 46.1 us -> none  [on_device(): norms = lax.all_gather(norm_grads[0].reshape(-1, 128), AXES, axis=0)]
    all_gather x1, waiting for transfers between devices: 0.01 us -> 16.9 us  [on_device(): gathered = lax.all_gather(base[None], AXES, axis=0, tiled=True)]
    pallas_call x1, Pallas kernels: 100 us -> 112 us  [rounds(): pl.pallas_call(functools.partial(rounds_kernel, sizes), out_shape=(jax.Sh...]
    unnamed x16 -> x8, local copies, waits for them, and re-layouts: 8.68 us -> 0.02 us
  transfers between devices with their start and end apart: 1 -> 1, of which waited for: 0 -> 1; matrix products, arithmetic and copies ran while one was open for 1% -> 2% of each run, Pallas kernels for 53% -> 68%
where the time goes in v2:
time: 164 us
  Pallas kernels  127 us (77%)
  waiting for transfers between devices  16.9 us (10%)
  between operations  14.1 us (9%)
  other arithmetic  4.1 us (2%)
    pallas_call x1, Pallas kernels, rounds(): pl.pallas_call(functools.partial(rounds_kernel, sizes), out_shape=(jax.Sh...  112 us
    all_gather x1, waiting for transfers between devices, on_device(): gathered = lax.all_gather(base[None], AXES, axis=0, tiled=True)  16.9 us
    pallas_call x1, Pallas kernels, finish(): pl.pallas_call(functools.partial(finish_kernel, per, slots), out_shape=(j...  15.6 us
  transfers between devices with their start and end apart: 1, of which 1 were waited for; matrix products, arithmetic and copies ran while one was open for 2% of the time, Pallas kernels for 68%

profile of v2, /device:TPU:0, one launch (start us, length us, event | category | flops | bytes accessed | tf_op | source)
XLA Modules:
  0.0 164.0 jit_solution(13288267844948013322)
XLA Ops:
  7.2 0.0 copy-start.3
  7.2 0.0 copy-start.1
  7.2 0.0 copy-start
  7.2 0.0 all-gather.2.cloned.1.call-start
  7.2 2.0 %multiply_subtract_fusion = f32[1,2,128,512]{3,2,1,0:T(8,128)} fusion(f32[1,2,128,512]{3,2,1,0:T(8,128)} %param.17, bf16[1,2,128,512]{3,2,1,0:T(8,128)(2,1)} %param.16), kind=kLoop, calls=%fused_computation | loop fusion | flops 393216 | bytes 1310720 | tf_op jit(solution)/shard_map/sub | solution.py:535
  9.2 0.0 all-gather.2.cloned.1.call-update
  9.2 1.3 reshape.40.norms
  10.6 111.9 %rounds.1 = (f32[2,32,2048]{2,1,0:T(8,128)}, f32[2,32,512]{2,1,0:T(8,128)}, f32[4,8,128]{2,1,0:T(8,128)}) custom-call(bf16[4096,512]{1,0:T(8,128)(2,1)} %bitcast.14, f32[4096,512]{1,0:T(8,128)} %bitcast.12, f32[2,32,512]{2,1,0:T(8,128)} %bitcast.17, f32[4,8,128]{2,1,0:T(8,128)} %reshape.40.norms), custom_call_target="tpu_custom_call" | custom-call | tf_op jit(solution)/shard_map/rounds/pallas_call | solution.py:403
  122.5 0.7 broadcast_multiply_fusion
  123.3 0.0 copy-done.3
  123.3 0.1 convert_reduce_fusion
  123.4 0.0 copy-start.2
  123.4 0.7 fusion.1.mine
  124.0 0.0 copy-done.1
  124.1 0.0 copy-done
  124.1 0.6 multiply_subtract_fusion.1
  124.7 16.9 %all-gather.2.cloned.1.call-done = f32[32,2,128,512]{3,2,1,0:T(8,128)} async-done(((f32[1,2,128,512]{3,2,1,0:T(8,128)}), f32[32,2,128,512]{3,2,1,0:T(8,128)}) %all-gather.2.cloned.1.call-update) | async-done | bytes 16777232 | tf_op jit(solution)/shard_map/all_gather | solution.py:536
  141.6 0.0 copy-done.2
  141.6 15.6 %finish.1 = (f32[4096,512]{1,0:T(8,128)}, bf16[4096,512]{1,0:T(8,128)(2,1)}, f32[2,128,512]{2,1,0:T(8,128)}) custom-call(s32[32]{0:T(128)} %copy-done.2, s32[2]{0:T(128)} %fusion.1.mine, f32[2,32,2048]{2,1,0:T(8,128)} %get-tuple-element.11.refs_0_, f32[2,32,512]{2,1,0:T(8,128)} %get-tuple-element.12.refs_1_, bf16[4096,512]{1,0:T(8,128)(2,1)} %bitcast.15, ...), custom_call_target="tpu_custom_call" | custom-call | tf_op jit(solution)/shard_map/finish/pallas_call | solution.py:489
  (3 shorter events, 0.0 us)
Async XLA Ops:
  7.2 116.1 %copy-start.3 = (s32[32]{0:T(128)S(1)}, s32[32]{0:T(128)}, u32[]{:S(2)}) copy-start(s32[32]{0:T(128)} %param.15) | copy-start | bytes 388
  7.2 116.9 %copy-start.1 = (f32[2,2048]{1,0:T(2,128)S(1)}, f32[2,2048]{1,0:T(2,128)}, u32[]{:S(2)}) copy-start(f32[2,2048]{1,0:T(2,128)} %param.14) | copy-start | bytes 49156
  7.2 116.9 %copy-start = (f32[2,2048]{1,0:T(2,128)S(1)}, f32[2,2048]{1,0:T(2,128)}, u32[]{:S(2)}) copy-start(f32[2,2048]{1,0:T(2,128)} %param.13) | copy-start | bytes 49156
  7.2 134.4 %all-gather.2.cloned.1.call-start = ((), (), s32[]{:S(2)}) async-start(), calls=%async_computation | async-start | bytes 17301504 | tf_op jit(solution)/shard_map/all_gather | solution.py:536
  123.4 18.2 %copy-start.2 = (s32[32]{0:T(128)}, s32[32]{0:T(128)S(1)}, u32[]{:S(2)}) copy-start(s32[32]{0:T(128)S(1)} %multiply_add_fusion.1.places) | copy-start | bytes 388
Sparse Core Ops, SparseCore 0:
  11.5 130.0 all-gather.1
